TPU v7x, 32 devices: a whole 2x2x4 slice. The times are simulated.
32 devices in a mesh: groups: 2 (over y), ctx: 4 (over z), dp: 2 (over x), mp: 2 (over core).
Axes of the slice: x: 2, y: 2, z: 4, core: 2. Of those that a mesh axis runs over, the one named last changes fastest.
Arguments:
- byte_ids: int32 [4, 1024], P(('groups', 'dp'), 'ctx'), parts along dimension 0, may hold values from 0 to 255
- lengths: int32 [4], P(('groups', 'dp')), parts along dimension 0, may hold values from 128 to 1024, as said below
- hidden: bfloat16 [4, 256, 768], P(('groups', 'dp'), 'ctx'), parts along dimension 0
- w_qkv: bfloat16 [768, 3, 768], P(None, None, 'mp'), may hold values from -0.21875 to 0.21875
- w_out: bfloat16 [768, 768], P('mp'), may hold values from -0.21875 to 0.21875
- w_up: bfloat16 [4, 768, 768], P(None, None, 'mp'), may hold values from -0.109375 to 0.109375
- w_head: bfloat16 [768, 256], P('mp'), may hold values from -0.21875 to 0.21875
Outputs:
- grad_hidden: bfloat16 [4, 256, 768], P(('groups', 'dp'), 'ctx'), parts along dimension 0
There are 2 independent parts, one for each index of `groups`. A program takes and returns all parts, laid end to end along the dimension named above; an argument that names none is the same for every part. Nothing has to cross between parts.
Inputs may be any that keep to these rules, and one draw needn't show every extreme that they name: `lengths`: each document's valid byte count; in every draw some document is full, with 1024 valid bytes.
All inputs are finite; a program needn't handle non-finite values.
Results may differ from a plain program's by a relative error of at most 0.025.
Values may be sent and summed in bfloat16 or wider, within the bound.
A program may use at most 64 MiB of HBM per device.

v0:
```python
import jax
import jax.numpy as jnp
from jax import lax
from jax.sharding import PartitionSpec as P

HEAD_DIM = 64


def with_halo(x, sides, width):
    for axis, dim in sides:
        devices, length = (lax.axis_size(axis), x.shape[dim])
        up = [(i, (i + 1) % devices) for i in range(devices - 1)]
        down = [(j, i) for i, j in up]
        last = lax.slice_in_dim(x, length - width, length, axis=dim)
        initial = lax.slice_in_dim(x, 0, width, axis=dim)
        before = lax.ppermute(last, axis, up)
        after = lax.ppermute(initial, axis, down)
        x = jnp.concatenate([before, x, after], axis=dim)
    return x


def pair_sum(values):
    return lax.psum(values, "mp")


def edges(values):
    return with_halo(values, (("ctx", 0),), 1)


def gelu_grad(pre_act, incoming):
    result, pullback = jax.vjp(jax.nn.gelu, pre_act)
    return pullback(incoming)[0]


def body(byte_ids, lengths, hidden, w_qkv, w_out, w_up, w_head):
    inputs = hidden[0]
    rows = inputs.shape[0]
    model_width = inputs.shape[1]
    split_width = w_qkv.shape[2]
    own_heads = split_width // HEAD_DIM
    scaling = HEAD_DIM ** (-0.5)
    length = lengths[0]
    my_first = lax.axis_index("ctx") * rows
    byte_rows = 4 * rows
    flat_qkv = w_qkv.reshape(model_width, 3 * split_width)
    projected = jnp.dot(inputs, flat_qkv, preferred_element_type=jnp.float32).astype(jnp.bfloat16)
    projected = projected.reshape(rows, 3, own_heads, HEAD_DIM)
    queries = projected[:, 0]
    key_rows = projected[:, 1]
    value_rows = projected[:, 2]

    def usable(first_row, count):
        return 4 * (first_row + jnp.arange(count, dtype=jnp.int32)) < length

    running = jnp.full((rows, own_heads), -1e30, jnp.float32)
    key_piece = lax.all_gather(key_rows, "ctx", axis=0, tiled=True)
    value_piece = lax.all_gather(value_rows, "ctx", axis=0, tiled=True)
    keep = usable(jnp.int32(0), key_piece.shape[0])[None, None, :]
    scores = (
        jnp.einsum("qhd,khd->qhk", queries, key_piece, preferred_element_type=jnp.float32) * scaling
    )
    newest = jnp.maximum(running, jnp.max(jnp.where(keep, scores, -1e30), axis=-1))
    weights = jnp.where(keep, jnp.exp(scores - newest[..., None]), 0.0)
    totals = jnp.sum(weights, axis=-1)
    weighted = jnp.einsum(
        "qhk,khd->qhd",
        weights.astype(jnp.bfloat16),
        value_piece,
        preferred_element_type=jnp.float32,
    )
    weighted, running, totals = (weighted, newest, totals)
    attn_heads = (weighted / totals[..., None]).astype(jnp.bfloat16)
    attn = attn_heads.reshape(rows, split_width)
    log_norm = running + jnp.log(totals)
    context = (
        inputs.astype(jnp.float32)
        + pair_sum(jnp.dot(attn, w_out, preferred_element_type=jnp.float32))
    ).astype(jnp.bfloat16)
    extended = edges(context)
    tap_outputs = [
        jnp.dot(extended, w_up[tap], preferred_element_type=jnp.float32) for tap in range(4)
    ]
    phases = []
    for phase in range(4):
        phase_sum = jnp.zeros((rows, split_width), jnp.float32)
        for tap in range(4):
            shifted = 1 + (phase + tap - 1) // 4
            phase_sum = phase_sum + tap_outputs[tap][shifted : shifted + rows]
        phases.append(phase_sum)
    pre_act = jnp.stack(phases, axis=1).reshape(byte_rows, split_width)
    activated = jax.nn.gelu(pre_act).astype(jnp.bfloat16)
    logits = pair_sum(jnp.dot(activated, w_head, preferred_element_type=jnp.float32))
    byte_first = lax.axis_index("ctx") * byte_rows
    byte_mask = byte_first + jnp.arange(byte_rows, dtype=jnp.int32) < length
    inverse = 1.0 / length.astype(jnp.float32)
    softmaxed = jax.nn.softmax(logits, axis=-1)
    onehot = (byte_ids[0][:, None] == jnp.arange(logits.shape[1], dtype=jnp.int32)[None, :]).astype(
        jnp.float32
    )
    logit_grad = ((softmaxed - onehot) * jnp.where(byte_mask, inverse, 0.0)[:, None]).astype(
        jnp.bfloat16
    )
    act_grad = jnp.dot(logit_grad, w_head.T, preferred_element_type=jnp.float32)
    pre_grad = gelu_grad(pre_act, act_grad).astype(jnp.bfloat16)
    grad_ext = edges(pre_grad.reshape(rows, 4 * split_width)).reshape(byte_rows + 8, split_width)
    partial_grad = jnp.zeros((rows, model_width), jnp.float32)
    for offset in range(4):
        window = grad_ext[5 - offset : 5 - offset + byte_rows].astype(jnp.float32)
        tap_sum = jnp.sum(window.reshape(rows, 4, split_width), axis=1).astype(jnp.bfloat16)
        partial_grad = partial_grad + jnp.dot(
            tap_sum, w_up[offset].T, preferred_element_type=jnp.float32
        )
    context_grad = pair_sum(partial_grad)
    attn_grad = jnp.dot(
        context_grad.astype(jnp.bfloat16), w_out.T, preferred_element_type=jnp.float32
    ).astype(jnp.bfloat16)
    attn_grad = attn_grad.reshape(rows, own_heads, HEAD_DIM)
    row_dots = jnp.sum(attn_grad.astype(jnp.float32) * attn_heads.astype(jnp.float32), axis=-1)
    key_piece = lax.all_gather(key_rows, "ctx", axis=0, tiled=True)
    value_piece = lax.all_gather(value_rows, "ctx", axis=0, tiled=True)
    keep = usable(jnp.int32(0), key_piece.shape[0])[None, None, :]
    scores = (
        jnp.einsum("qhd,khd->qhk", queries, key_piece, preferred_element_type=jnp.float32) * scaling
    )
    probs = jnp.where(keep, jnp.exp(scores - log_norm[..., None]), 0.0)
    product = jnp.einsum("qhd,khd->qhk", attn_grad, value_piece, preferred_element_type=jnp.float32)
    score_grad = (probs * (product - row_dots[..., None])).astype(jnp.bfloat16)
    query_sum = jnp.einsum(
        "qhk,khd->qhd", score_grad, key_piece, preferred_element_type=jnp.float32
    )
    query_grad = (query_sum * scaling).astype(jnp.bfloat16)
    key_keep = usable(my_first, rows)[None, None, :]
    norm_all, dots_all = (
        lax.all_gather(log_norm, "ctx", axis=0, tiled=True),
        lax.all_gather(row_dots, "ctx", axis=0, tiled=True),
    )
    query_piece = lax.all_gather(queries, "ctx", axis=0, tiled=True)
    outgrad_piece = lax.all_gather(attn_grad, "ctx", axis=0, tiled=True)
    count = query_piece.shape[0]
    scores = (
        jnp.einsum("qhd,khd->qhk", query_piece, key_rows, preferred_element_type=jnp.float32)
        * scaling
    )
    probs = jnp.where(key_keep, jnp.exp(scores - norm_all[..., None]), 0.0)
    product = jnp.einsum(
        "qhd,khd->qhk", outgrad_piece, value_rows, preferred_element_type=jnp.float32
    )
    score_grad = (probs * (product - dots_all[..., None])).astype(jnp.bfloat16)
    key_sum = jnp.einsum(
        "qhk,qhd->khd", score_grad, query_piece, preferred_element_type=jnp.float32
    )
    value_sum = jnp.einsum(
        "qhk,qhd->khd",
        probs.astype(jnp.bfloat16),
        outgrad_piece,
        preferred_element_type=jnp.float32,
    )
    key_sum, value_sum = (key_sum, value_sum)
    key_grad = (key_sum * scaling).astype(jnp.bfloat16)
    value_grad = value_sum.astype(jnp.bfloat16)
    stacked = jnp.stack([query_grad, key_grad, value_grad], axis=1).reshape(rows, 3 * split_width)
    back_proj = pair_sum(jnp.dot(stacked, flat_qkv.T, preferred_element_type=jnp.float32))
    input_grad = (context_grad + back_proj).astype(jnp.bfloat16)
    return input_grad[None]


def solution(mesh):
    placed = (
        P(("groups", "dp"), "ctx"),
        P(("groups", "dp")),
        P(("groups", "dp"), "ctx", None),
        P(None, None, "mp"),
        P("mp", None),
        P(None, None, "mp"),
        P("mp", None),
    )
    return jax.shard_map(
        body,
        mesh=mesh,
        in_specs=placed,
        out_specs=P(("groups", "dp"), "ctx", None),
        check_vma=False,
    )
```

profile of v0, /device:TPU:0, one launch (start us, length us, event | category | flops | bytes accessed | tf_op | source)
XLA Modules:
  0.0 255.1 jit_solution(12642925866357019696)
XLA Ops:
  7.3 2.6 %copy.24 = bf16[768,3,384]{0,2,1:T(8,128)(2,1)S(1)} copy(bf16[768,3,384]{2,0,1:T(8,128)(2,1)} %param.10) | data formatting | bytes 3538944 | tf_op args[3]
  12.2 17.3 %all-gather.1 = bf16[256,1,6,64]{3,2,1,0:T(8,128)(2,1)S(1)} all-gather(bf16[64,1,6,64]{3,2,1,0:T(8,128)(2,1)S(1)} %get-tuple-element.11), channel_id=3, replica_groups=mesh['groups'=2,'ctx'=4,'dp'=2,'mp'=2] {'ctx'}, dimensions={0}, use_global_device_ids=true | all-gather | bytes 245760 | tf_op jit(solution)/shard_map/all_gather | solution.py:56
  32.7 16.3 %all-gather = bf16[256,1,6,64]{3,2,1,0:T(8,128)(2,1)S(1)} all-gather(bf16[64,1,6,64]{3,2,1,0:T(8,128)(2,1)S(1)} %get-tuple-element.9), channel_id=2, replica_groups=mesh['groups'=2,'ctx'=4,'dp'=2,'mp'=2] {'ctx'}, dimensions={0}, use_global_device_ids=true | all-gather | bytes 245760 | tf_op jit(solution)/shard_map/all_gather | solution.py:57
  52.5 18.5 %all-reduce.5.cloned.1.call-done = f32[64,768]{1,0:T(8,128)} async-done(((f32[64,768]{1,0:T(8,128)}), f32[64,768]{1,0:T(8,128)}) %all-reduce.5.cloned.1.call-update) | async-done | bytes 196624 | tf_op jit(solution)/shard_map/psum | solution.py:23
  72.0 3.6 %collective-permute-start = (bf16[1,768]{1,0:T(2,128)(2,1)S(1)}, bf16[1,768]{1,0:T(2,128)(2,1)S(1)}, u32[]{:S(2)}, u32[]{:S(2)}) collective-permute-start(bf16[1,768]{1,0:T(2,128)(2,1)S(1)} %get-tuple-element.17), channel_id=1, source_target_pairs={{0,4},{4,8},{8,12},{1,5},{5,9},{9,13},{2,6},{6,10},{10,14},{3,7},{... | collective-permute-start | bytes 4616 | tf_op jit(solution)/shard_map/ppermute | solution.py:16
  75.6 1.3 collective-permute-start.1
  77.0 4.2 %collective-permute-done.1 = bf16[1,768]{1,0:T(2,128)(2,1)S(1)} collective-permute-done((bf16[1,768]{1,0:T(2,128)(2,1)S(1)}, bf16[1,768]{1,0:T(2,128)(2,1)S(1)}, u32[]{:S(2)}, u32[]{:S(2)}) %collective-permute-start.1) | collective-permute-done | bytes 1568 | tf_op jit(solution)/shard_map/ppermute | solution.py:17
  81.1 1.3 fusion.22
  82.4 1.3 fusion.19
  83.8 1.3 fusion.29
  85.1 1.3 fusion.85
  87.6 2.0 fusion.67
  90.2 17.8 %all-reduce.7.cloned.1.call-done = f32[256,256]{1,0:T(8,128)} async-done(((f32[256,256]{1,0:T(8,128)}), f32[256,256]{1,0:T(8,128)}) %all-reduce.7.cloned.1.call-update) | async-done | bytes 262160 | tf_op jit(solution)/shard_map/psum | solution.py:23
  110.2 1.6 fusion.45
  111.9 4.2 %collective-permute-start.2 = (bf16[1,1536]{1,0:T(2,128)(2,1)S(1)}, bf16[1,1536]{1,0:T(2,128)(2,1)}, u32[]{:S(2)}, u32[]{:S(2)}) collective-permute-start(bf16[1,1536]{1,0:T(2,128)(2,1)S(1)} %bitcast.170), channel_id=1, source_target_pairs={{0,4},{4,8},{8,12},{1,5},{5,9},{9,13},{2,6},{6,10},{10,14},{3,7},{... | collective-permute-start | bytes 9224 | tf_op jit(solution)/shard_map/ppermute | solution.py:16
  118.0 15.7 %all-gather.2 = bf16[256,1,6,64]{3,0,2,1:T(8,128)(2,1)S(1)} all-gather(bf16[64,1,6,64]{3,0,2,1:T(8,128)(2,1)S(1)} %copy.46), channel_id=4, replica_groups=mesh['groups'=2,'ctx'=4,'dp'=2,'mp'=2] {'ctx'}, dimensions={0}, use_global_device_ids=true | all-gather | bytes 245760 | tf_op jit(solution)/shard_map/all_gather | solution.py:137
  133.7 13.4 %all-gather.3 = f32[4,64,6]{1,2,0:T(8,128)S(1)} all-gather(f32[1,64,6]{1,2,0:T(8,128)S(1)} %bitcast.168), channel_id=1, replica_groups=mesh['groups'=2,'ctx'=4,'dp'=2,'mp'=2] {'ctx'}, dimensions={0}, use_global_device_ids=true | all-gather | bytes 7680 | tf_op jit(solution)/shard_map/all_gather | solution.py:134
  148.1 1.8 reduce_sum.69
  149.8 1.4 pad_maximum_fusion.2
  155.1 2.1 fusion.27
  159.3 1.4 convolution_add_fusion.2
  160.7 1.4 convolution_add_fusion.1
  162.2 2.1 convolution_add_fusion
  165.5 18.4 %all-reduce.9.cloned.1.call-done = f32[64,768]{1,0:T(8,128)} async-done(((f32[64,768]{1,0:T(8,128)}), f32[64,768]{1,0:T(8,128)}) %all-reduce.9.cloned.1.call-update) | async-done | bytes 196624 | tf_op jit(solution)/shard_map/psum | solution.py:23
  183.9 1.9 convolution_convert_fusion.2
  185.7 1.5 copy.33
  188.2 1.7 copy.37
  189.9 2.1 fusion.16
  192.0 13.4 %all-gather.4 = f32[4,64,6]{1,2,0:T(8,128)S(1)} all-gather(f32[1,64,6]{1,2,0:T(8,128)S(1)} %bitcast.169), channel_id=1, replica_groups=mesh['groups'=2,'ctx'=4,'dp'=2,'mp'=2] {'ctx'}, dimensions={0}, use_global_device_ids=true | all-gather | bytes 7680 | tf_op jit(solution)/shard_map/all_gather | solution.py:135
  205.5 17.8 %all_gather.24 = bf16[256,6,64]{2,1,0:T(8,128)(2,1)} all-gather(bf16[64,6,64]{2,1,0:T(8,128)(2,1)} %copy.37), channel_id=1, replica_groups=mesh['groups'=2,'ctx'=4,'dp'=2,'mp'=2] {'ctx'}, dimensions={0}, use_global_device_ids=true | all-gather | bytes 245760 | tf_op jit(solution)/shard_map/all_gather | solution.py:138
  228.9 18.0 %all-reduce.11.cloned.1.call-done = f32[64,768]{1,0:T(8,128)} async-done(((f32[64,768]{1,0:T(8,128)}), f32[64,768]{1,0:T(8,128)}) %all-reduce.11.cloned.1.call-update) | async-done | bytes 196624 | tf_op jit(solution)/shard_map/psum | solution.py:23
  246.9 1.7 fusion.75
  (78 shorter events, 30.3 us)
Async XLA Ops:
  6.5 44.9 %copy-start = (bf16[384,768]{1,0:T(8,128)(2,1)S(1)}, bf16[384,768]{1,0:T(8,128)(2,1)}, u32[]{:S(2)}) copy-start(bf16[384,768]{1,0:T(8,128)(2,1)} %param.11) | copy-start | bytes 1769476
  6.5 3.4 %copy-start.3 = (bf16[1,64,768]{2,1,0:T(8,128)(2,1)S(1)}, bf16[1,64,768]{2,1,0:T(8,128)(2,1)}, u32[]{:S(2)}) copy-start(bf16[1,64,768]{2,1,0:T(8,128)(2,1)} %param.9) | copy-start | bytes 294916
  6.5 64.5 %all-reduce.5.cloned.1.call-start = ((), (), s32[]{:S(2)}) async-start(), calls=%async_computation | async-start | bytes 393216 | tf_op jit(solution)/shard_map/psum | solution.py:23
  7.3 42.9 %copy-start.8 = (pred[256]{0:T(512)(128)(4,1)}, pred[256]{0:T(512)(128)(4,1)S(1)}, u32[]{:S(2)}) copy-start(pred[256]{0:T(512)(128)(4,1)S(1)} %multiply_compare_fusion) | copy-start | bytes 772
  11.6 0.7 copy-start.2
  11.6 39.8 %copy-start.1 = (bf16[64,1,6,64]{3,2,1,0:T(8,128)(2,1)}, bf16[64,1,6,64]{3,2,1,0:T(8,128)(2,1)S(1)}, u32[]{:S(2)}) copy-start(bf16[64,1,6,64]{3,2,1,0:T(8,128)(2,1)S(1)} %get-tuple-element.9) | copy-start | bytes 147460
  49.9 21.1 %copy-start.4 = (bf16[1,64,768]{2,1,0:T(8,128)(2,1)S(1)}, bf16[1,64,768]{2,1,0:T(8,128)(2,1)}, u32[]{:S(2)}) copy-start(bf16[1,64,768]{2,1,0:T(8,128)(2,1)} %param.9) | copy-start | bytes 294916
  51.4 35.0 %copy-start.5 = (bf16[64,6,64]{0,2,1:T(8,128)(2,1)}, bf16[64,6,64]{0,2,1:T(8,128)(2,1)S(1)}, u32[]{:S(2)}) copy-start(bf16[64,6,64]{0,2,1:T(8,128)(2,1)S(1)} %fusion.12) | copy-start | bytes 147460
  52.4 55.6 %all-reduce.7.cloned.1.call-start = ((), (), s32[]{:S(2)}) async-start(), calls=%async_computation.1 | async-start | bytes 524288 | tf_op jit(solution)/shard_map/psum | solution.py:23
  72.0 5.0 %collective-permute-start = (bf16[1,768]{1,0:T(2,128)(2,1)S(1)}, bf16[1,768]{1,0:T(2,128)(2,1)S(1)}, u32[]{:S(2)}, u32[]{:S(2)}) collective-permute-start(bf16[1,768]{1,0:T(2,128)(2,1)S(1)} %get-tuple-element.17), channel_id=1, source_target_pairs={{0,4},{4,8},{8,12},{1,5},{5,9},{9,13},{2,6},{6,10},{10,14},{3,7},{... | collective-permute-start | bytes 4616 | tf_op jit(solution)/shard_map/ppermute | solution.py:16
  75.6 5.5 %collective-permute-start.1 = (bf16[1,768]{1,0:T(2,128)(2,1)S(1)}, bf16[1,768]{1,0:T(2,128)(2,1)S(1)}, u32[]{:S(2)}, u32[]{:S(2)}) collective-permute-start(bf16[1,768]{1,0:T(2,128)(2,1)S(1)} %get-tuple-element.18), channel_id=1, source_target_pairs={{4,0},{8,4},{12,8},{5,1},{9,5},{13,9},{6,2},{10,6},{14,10},{7,3},{... | collective-permute-start | bytes 4616 | tf_op jit(solution)/shard_map/ppermute | solution.py:17
  86.4 23.8 %copy-start.9 = (s32[1,256]{1,0:T(1,128)S(1)}, s32[1,256]{1,0:T(1,128)}, u32[]{:S(2)}) copy-start(s32[1,256]{1,0:T(1,128)} %param.7) | copy-start | bytes 3076
  89.6 94.2 %all-reduce.9.cloned.1.call-start = ((), (), s32[]{:S(2)}) async-start(), calls=%async_computation.2 | async-start | bytes 393216 | tf_op jit(solution)/shard_map/psum | solution.py:23
  90.2 43.5 %copy-start.6 = (f32[64,6]{0,1:T(8,128)}, f32[64,6]{0,1:T(8,128)S(1)}, u32[]{:S(2)}) copy-start(f32[64,6]{0,1:T(8,128)S(1)} %log_add_fusion) | copy-start | bytes 4612
  111.9 37.9 %collective-permute-start.2 = (bf16[1,1536]{1,0:T(2,128)(2,1)S(1)}, bf16[1,1536]{1,0:T(2,128)(2,1)}, u32[]{:S(2)}, u32[]{:S(2)}) collective-permute-start(bf16[1,1536]{1,0:T(2,128)(2,1)S(1)} %bitcast.170), channel_id=1, source_target_pairs={{0,4},{4,8},{8,12},{1,5},{5,9},{9,13},{2,6},{6,10},{10,14},{3,7},{... | collective-permute-start | bytes 9224 | tf_op jit(solution)/shard_map/ppermute | solution.py:16
  116.8 33.1 %collective-permute-start.3 = (bf16[1,1536]{1,0:T(2,128)(2,1)}, bf16[1,1536]{1,0:T(2,128)(2,1)}, u32[]{:S(2)}, u32[]{:S(2)}) collective-permute-start(bf16[1,1536]{1,0:T(2,128)(2,1)} %bitcast.43), channel_id=1, source_target_pairs={{4,0},{8,4},{12,8},{5,1},{9,5},{13,9},{6,2},{10,6},{14,10},{7,3},{... | collective-permute-start | bytes 9224 | tf_op jit(solution)/shard_map/ppermute | solution.py:17
  160.7 29.2 %copy-start.7 = (f32[64,6]{0,1:T(8,128)S(1)}, f32[64,6]{0,1:T(8,128)}, u32[]{:S(2)}) copy-start(f32[64,6]{0,1:T(8,128)} %copy-done.6) | copy-start | bytes 4612
  164.2 82.7 %all-reduce.11.cloned.1.call-start = ((), (), s32[]{:S(2)}) async-start(), calls=%async_computation.3 | async-start | bytes 393216 | tf_op jit(solution)/shard_map/psum | solution.py:23
Sparse Core Ops, SparseCore 0:
  52.5 18.4 all-reduce.4
  89.8 18.2 all-reduce.6
  164.4 19.4 all-reduce.8
  229.0 17.8 all-reduce.10
where the time goes:
time: 256 us; the launch traced here: 255 us
  blocking collectives  93.9 us (37%)
  waiting for transfers between devices  77 us (30%)
  matrix products  28.3 us (11%)
  local copies, waits for them, and re-layouts  18.3 us (7%)
  between operations  14.2 us (6%)
  other arithmetic  12.9 us (5%)
  starting transfers between devices  10.6 us (4%)
    psum x4, waiting for transfers between devices, pair_sum(): return lax.psum(values, 'mp')  72.7 us
    all_gather x1, blocking collectives, body(): outgrad_piece = lax.all_gather(attn_grad, 'ctx', axis=0, tiled=True)  17.8 us
    all_gather x1, blocking collectives, body(): key_piece = lax.all_gather(key_rows, 'ctx', axis=0, tiled=True)  17.3 us
    all_gather x1, blocking collectives, body(): value_piece = lax.all_gather(value_rows, 'ctx', axis=0, tiled=True)  16.3 us
    all_gather x1, blocking collectives, body(): query_piece = lax.all_gather(queries, 'ctx', axis=0, tiled=True)  15.7 us
    all_gather x1, blocking collectives, body(): lax.all_gather(row_dots, 'ctx', axis=0, tiled=True)  13.4 us
    all_gather x1, blocking collectives, body(): lax.all_gather(log_norm, 'ctx', axis=0, tiled=True)  13.4 us
    ppermute x2, starting transfers between devices, with_halo(): before = lax.ppermute(last, axis, up)  7.88 us
  transfers between devices with their start and end apart: 8, of which 5 were waited for; matrix products, arithmetic and copies ran while one was open for 2% of the time, Pallas kernels for 0%

commit v1 on v0

--- a/solution.py
+++ b/solution.py
@@ -135,7 +135,12 @@
         lax.all_gather(row_dots, "ctx", axis=0, tiled=True),
     )
     query_piece = lax.all_gather(queries, "ctx", axis=0, tiled=True)
-    outgrad_piece = lax.all_gather(attn_grad, "ctx", axis=0, tiled=True)
+    ring = [attn_grad]
+    for hop in range(3):
+        ring.append(lax.ppermute(ring[-1], "ctx", [(dev, (dev + 1) % 4) for dev in range(4)]))
+    outgrad_piece = jnp.roll(
+        jnp.concatenate(ring[::-1], axis=0), (lax.axis_index("ctx") + 1) * ring[0].shape[0], axis=0
+    )
     count = query_piece.shape[0]
     scores = (
         jnp.einsum("qhd,khd->qhk", query_piece, key_rows, preferred_element_type=jnp.float32)

time: 256 us -> 224 us (0.88)
  blocking collectives: 93.9 us -> 74.5 us
  local copies, waits for them, and re-layouts: 18.3 us -> 13.5 us
  other arithmetic: 12.9 us -> 8.83 us
    all_gather x1 -> x0, blocking collectives: 17.8 us -> none  [body(): outgrad_piece = lax.all_gather(attn_grad, 'ctx', axis=0, tiled=True)]
    psum x4, waiting for transfers between devices: 72.7 us -> 56.5 us  [pair_sum(): return lax.psum(values, 'mp')]
    ppermute x0 -> x3, waiting for transfers between devices: none -> 11.1 us  [body(): lax.ppermute(ring[-1], 'ctx', [(dev, (dev + 1) % 4) for dev in range(4)])]
    ppermute x2, waiting for transfers between devices: 4.16 us -> 7.95 us  [with_halo(): after = lax.ppermute(initial, axis, down)]
    reduce_sum x4, other arithmetic: 3.75 us -> 0.97 us  [body(): jnp.sum(window.reshape(rows, 4, split_width), axis=1).astype(jnp.bfloat16)]
  transfers between devices with their start and end apart: 8 -> 11, of which waited for: 5 -> 7; matrix products, arithmetic and copies ran while one was open for 2% -> 2% of each run, Pallas kernels for 0% -> 0%
where the time goes in v1:
time: 224 us; the launch traced here: 223 us
  waiting for transfers between devices  75.6 us (34%)
  blocking collectives  74.5 us (33%)
  matrix products  26.2 us (12%)
  between operations  14.4 us (6%)
  local copies, waits for them, and re-layouts  13.5 us (6%)
  starting transfers between devices  10.2 us (5%)
  other arithmetic  8.83 us (4%)
    psum x4, waiting for transfers between devices, pair_sum(): return lax.psum(values, 'mp')  56.5 us
    all_gather x1, blocking collectives, body(): key_piece = lax.all_gather(key_rows, 'ctx', axis=0, tiled=True)  17.3 us
    all_gather x1, blocking collectives, body(): value_piece = lax.all_gather(value_rows, 'ctx', axis=0, tiled=True)  16.3 us
    all_gather x1, blocking collectives, body(): query_piece = lax.all_gather(queries, 'ctx', axis=0, tiled=True)  14.5 us
    all_gather x1, blocking collectives, body(): lax.all_gather(log_norm, 'ctx', axis=0, tiled=True)  13.2 us
    all_gather x1, blocking collectives, body(): lax.all_gather(row_dots, 'ctx', axis=0, tiled=True)  13.1 us
    ppermute x3, waiting for transfers between devices, body(): lax.ppermute(ring[-1], 'ctx', [(dev, (dev + 1) % 4) for dev in range(4)])  11.1 us
    ppermute x2, waiting for transfers between devices, with_halo(): after = lax.ppermute(initial, axis, down)  7.95 us
  transfers between devices with their start and end apart: 11, of which 7 were waited for; matrix products, arithmetic and copies ran while one was open for 2% of the time, Pallas kernels for 0%

profile of v1, /device:TPU:0, one launch (start us, length us, event | category | flops | bytes accessed | tf_op | source)
XLA Modules:
  0.0 223.1 jit_solution(1445534484856100438)
XLA Ops:
  7.3 2.6 %copy.24 = bf16[768,3,384]{0,2,1:T(8,128)(2,1)S(1)} copy(bf16[768,3,384]{2,0,1:T(8,128)(2,1)} %param.10) | data formatting | bytes 3538944 | tf_op args[3]
  12.2 17.3 %all-gather.1 = bf16[256,1,6,64]{3,2,1,0:T(8,128)(2,1)S(1)} all-gather(bf16[64,1,6,64]{3,2,1,0:T(8,128)(2,1)S(1)} %get-tuple-element.11), channel_id=3, replica_groups=mesh['groups'=2,'ctx'=4,'dp'=2,'mp'=2] {'ctx'}, dimensions={0}, use_global_device_ids=true | all-gather | bytes 245760 | tf_op jit(solution)/shard_map/all_gather | solution.py:56
  31.4 1.2 select_reduce_fusion
  33.2 16.3 %all-gather = bf16[256,1,6,64]{3,2,1,0:T(8,128)(2,1)S(1)} all-gather(bf16[64,1,6,64]{3,2,1,0:T(8,128)(2,1)S(1)} %get-tuple-element.9), channel_id=2, replica_groups=mesh['groups'=2,'ctx'=4,'dp'=2,'mp'=2] {'ctx'}, dimensions={0}, use_global_device_ids=true | all-gather | bytes 245760 | tf_op jit(solution)/shard_map/all_gather | solution.py:57
  50.8 1.2 fusion.12
  53.0 18.6 %all-reduce.5.cloned.1.call-done = f32[64,768]{1,0:T(8,128)} async-done(((f32[64,768]{1,0:T(8,128)}), f32[64,768]{1,0:T(8,128)}) %all-reduce.5.cloned.1.call-update) | async-done | bytes 196624 | tf_op jit(solution)/shard_map/psum | solution.py:23
  72.7 3.6 %collective-permute-start = (bf16[1,768]{1,0:T(2,128)(2,1)S(1)}, bf16[1,768]{1,0:T(2,128)(2,1)S(1)}, u32[]{:S(2)}, u32[]{:S(2)}) collective-permute-start(bf16[1,768]{1,0:T(2,128)(2,1)S(1)} %get-tuple-element.17), channel_id=1, source_target_pairs={{0,4},{4,8},{8,12},{1,5},{5,9},{9,13},{2,6},{6,10},{10,14},{3,7},{... | collective-permute-start | bytes 4616 | tf_op jit(solution)/shard_map/ppermute | solution.py:16
  76.4 1.3 collective-permute-start.1
  77.7 4.2 %collective-permute-done.1 = bf16[1,768]{1,0:T(2,128)(2,1)S(1)} collective-permute-done((bf16[1,768]{1,0:T(2,128)(2,1)S(1)}, bf16[1,768]{1,0:T(2,128)(2,1)S(1)}, u32[]{:S(2)}, u32[]{:S(2)}) %collective-permute-start.1) | collective-permute-done | bytes 1568 | tf_op jit(solution)/shard_map/ppermute | solution.py:17
  81.9 1.3 fusion.22
  83.2 1.3 fusion.19
  86.2 2.0 fusion.67
  88.4 18.3 %all-reduce.7.cloned.1.call-done = f32[256,256]{1,0:T(8,128)} async-done(((f32[256,256]{1,0:T(8,128)}), f32[256,256]{1,0:T(8,128)}) %all-reduce.7.cloned.1.call-update) | async-done | bytes 262160 | tf_op jit(solution)/shard_map/psum | solution.py:23
  108.9 1.6 fusion.45
  110.5 3.6 %collective-permute-start.2 = (bf16[1,1536]{1,0:T(2,128)(2,1)S(1)}, bf16[1,1536]{1,0:T(2,128)(2,1)S(1)}, u32[]{:S(2)}, u32[]{:S(2)}) collective-permute-start(bf16[1,1536]{1,0:T(2,128)(2,1)S(1)} %bitcast.165), channel_id=1, source_target_pairs={{0,4},{4,8},{8,12},{1,5},{5,9},{9,13},{2,6},{6,10},{10,14},{3,7},{... | collective-permute-start | bytes 9224 | tf_op jit(solution)/shard_map/ppermute | solution.py:16
  114.2 1.3 collective-permute-start.3
  116.0 3.8 %collective-permute-done.3 = bf16[1,1536]{1,0:T(2,128)(2,1)S(1)} collective-permute-done((bf16[1,1536]{1,0:T(2,128)(2,1)S(1)}, bf16[1,1536]{1,0:T(2,128)(2,1)S(1)}, u32[]{:S(2)}, u32[]{:S(2)}) %collective-permute-start.3) | collective-permute-done | bytes 3104 | tf_op jit(solution)/shard_map/ppermute | solution.py:17
  122.0 2.0 fusion.27
  124.6 1.4 convolution_add_fusion.2
  126.0 1.4 convolution_add_fusion.1
  127.4 2.1 convolution_add_fusion
  129.6 13.2 %all-gather.3 = f32[4,64,6]{1,2,0:T(8,128)S(1)} all-gather(f32[1,64,6]{1,2,0:T(8,128)S(1)} %bitcast.163), channel_id=1, replica_groups=mesh['groups'=2,'ctx'=4,'dp'=2,'mp'=2] {'ctx'}, dimensions={0}, use_global_device_ids=true | all-gather | bytes 7680 | tf_op jit(solution)/shard_map/all_gather | solution.py:134
  142.9 14.5 %all-gather.2 = bf16[256,1,6,64]{3,0,2,1:T(8,128)(2,1)S(1)} all-gather(bf16[64,1,6,64]{3,0,2,1:T(8,128)(2,1)S(1)} %copy.43), channel_id=4, replica_groups=mesh['groups'=2,'ctx'=4,'dp'=2,'mp'=2] {'ctx'}, dimensions={0}, use_global_device_ids=true | all-gather | bytes 245760 | tf_op jit(solution)/shard_map/all_gather | solution.py:137
  157.9 1.2 convolution_convert_fusion.2
  161.3 5.3 %collective-permute-done.4 = bf16[64,6,64]{0,2,1:T(8,128)(2,1)} collective-permute-done((bf16[64,6,64]{0,2,1:T(8,128)(2,1)}, bf16[64,6,64]{0,2,1:T(8,128)(2,1)}, u32[]{:S(2)}, u32[]{:S(2)}) %collective-permute-start.4) | collective-permute-done | bytes 49184 | tf_op jit(solution)/shard_map/ppermute | solution.py:140
  167.6 5.8 %collective-permute-done.5 = bf16[64,6,64]{0,2,1:T(8,128)(2,1)} collective-permute-done((bf16[64,6,64]{0,2,1:T(8,128)(2,1)}, bf16[64,6,64]{0,2,1:T(8,128)(2,1)}, u32[]{:S(2)}, u32[]{:S(2)}) %collective-permute-start.5) | collective-permute-done | bytes 49184 | tf_op jit(solution)/shard_map/ppermute | solution.py:140
  173.4 2.1 fusion.16
  175.5 13.1 %all-gather.4 = f32[4,64,6]{1,2,0:T(8,128)S(1)} all-gather(f32[1,64,6]{1,2,0:T(8,128)S(1)} %bitcast.164), channel_id=1, replica_groups=mesh['groups'=2,'ctx'=4,'dp'=2,'mp'=2] {'ctx'}, dimensions={0}, use_global_device_ids=true | all-gather | bytes 7680 | tf_op jit(solution)/shard_map/all_gather | solution.py:135
  188.8 1.5 concatenate.14
  191.2 2.0 fusion.15
  195.4 19.6 %all-reduce.11.cloned.1.call-done = f32[64,768]{1,0:T(8,128)} async-done(((f32[64,768]{1,0:T(8,128)}), f32[64,768]{1,0:T(8,128)}) %all-reduce.11.cloned.1.call-update) | async-done | bytes 196624 | tf_op jit(solution)/shard_map/psum | solution.py:23
  215.0 1.6 fusion.78
  (92 shorter events, 22.3 us)
Async XLA Ops:
  6.5 45.5 %copy-start = (bf16[384,768]{1,0:T(8,128)(2,1)S(1)}, bf16[384,768]{1,0:T(8,128)(2,1)}, u32[]{:S(2)}) copy-start(bf16[384,768]{1,0:T(8,128)(2,1)} %param.11) | copy-start | bytes 1769476
  6.5 3.4 %copy-start.5 = (bf16[1,64,768]{2,1,0:T(8,128)(2,1)S(1)}, bf16[1,64,768]{2,1,0:T(8,128)(2,1)}, u32[]{:S(2)}) copy-start(bf16[1,64,768]{2,1,0:T(8,128)(2,1)} %param.9) | copy-start | bytes 294916
  6.5 65.1 %all-reduce.5.cloned.1.call-start = ((), (), s32[]{:S(2)}) async-start(), calls=%async_computation | async-start | bytes 393216 | tf_op jit(solution)/shard_map/psum | solution.py:23
  7.3 43.5 %copy-start.12 = (pred[256]{0:T(512)(128)(4,1)}, pred[256]{0:T(512)(128)(4,1)S(1)}, u32[]{:S(2)}) copy-start(pred[256]{0:T(512)(128)(4,1)S(1)} %multiply_compare_fusion) | copy-start | bytes 772
  11.6 0.6 copy-start.3
  11.6 40.4 %copy-start.2 = (bf16[64,1,6,64]{3,2,1,0:T(8,128)(2,1)}, bf16[64,1,6,64]{3,2,1,0:T(8,128)(2,1)S(1)}, u32[]{:S(2)}) copy-start(bf16[64,1,6,64]{3,2,1,0:T(8,128)(2,1)S(1)} %get-tuple-element.9) | copy-start | bytes 147460
  32.6 0.6 copy-start.8
  50.5 21.1 %copy-start.6 = (bf16[1,64,768]{2,1,0:T(8,128)(2,1)S(1)}, bf16[1,64,768]{2,1,0:T(8,128)(2,1)}, u32[]{:S(2)}) copy-start(bf16[1,64,768]{2,1,0:T(8,128)(2,1)} %param.9) | copy-start | bytes 294916
  50.7 2.3 %copy-start.10 = (f32[64,6]{0,1:T(8,128)}, f32[64,6]{0,1:T(8,128)S(1)}, u32[]{:S(2)}) copy-start(f32[64,6]{0,1:T(8,128)S(1)} %fusion.51) | copy-start | bytes 4612
  52.0 33.0 %copy-start.7 = (bf16[64,6,64]{0,2,1:T(8,128)(2,1)}, bf16[64,6,64]{0,2,1:T(8,128)(2,1)S(1)}, u32[]{:S(2)}) copy-start(bf16[64,6,64]{0,2,1:T(8,128)(2,1)S(1)} %fusion.12) | copy-start | bytes 147460
  53.0 53.7 %all-reduce.7.cloned.1.call-start = ((), (), s32[]{:S(2)}) async-start(), calls=%async_computation.1 | async-start | bytes 524288 | tf_op jit(solution)/shard_map/psum | solution.py:23
  71.6 12.9 %copy-start.1 = (bf16[4,768,384]{2,1,0:T(8,128)(2,1)S(1)}, bf16[4,768,384]{2,1,0:T(8,128)(2,1)}, u32[]{:S(2)}) copy-start(bf16[4,768,384]{2,1,0:T(8,128)(2,1)} %param.12) | copy-start | bytes 7077892
  72.7 5.0 %collective-permute-start = (bf16[1,768]{1,0:T(2,128)(2,1)S(1)}, bf16[1,768]{1,0:T(2,128)(2,1)S(1)}, u32[]{:S(2)}, u32[]{:S(2)}) collective-permute-start(bf16[1,768]{1,0:T(2,128)(2,1)S(1)} %get-tuple-element.17), channel_id=1, source_target_pairs={{0,4},{4,8},{8,12},{1,5},{5,9},{9,13},{2,6},{6,10},{10,14},{3,7},{... | collective-permute-start | bytes 4616 | tf_op jit(solution)/shard_map/ppermute | solution.py:16
  76.4 5.5 %collective-permute-start.1 = (bf16[1,768]{1,0:T(2,128)(2,1)S(1)}, bf16[1,768]{1,0:T(2,128)(2,1)S(1)}, u32[]{:S(2)}, u32[]{:S(2)}) collective-permute-start(bf16[1,768]{1,0:T(2,128)(2,1)S(1)} %get-tuple-element.18), channel_id=1, source_target_pairs={{4,0},{8,4},{12,8},{5,1},{9,5},{13,9},{6,2},{10,6},{14,10},{7,3},{... | collective-permute-start | bytes 4616 | tf_op jit(solution)/shard_map/ppermute | solution.py:17
  85.0 23.8 %copy-start.14 = (s32[1,256]{1,0:T(1,128)S(1)}, s32[1,256]{1,0:T(1,128)}, u32[]{:S(2)}) copy-start(s32[1,256]{1,0:T(1,128)} %param.7) | copy-start | bytes 3076
  88.3 69.7 %all-reduce.9.cloned.1.call-start = ((), (), s32[]{:S(2)}) async-start(), calls=%async_computation.2 | async-start | bytes 393216 | tf_op jit(solution)/shard_map/psum | solution.py:23
  110.5 5.4 %collective-permute-start.2 = (bf16[1,1536]{1,0:T(2,128)(2,1)S(1)}, bf16[1,1536]{1,0:T(2,128)(2,1)S(1)}, u32[]{:S(2)}, u32[]{:S(2)}) collective-permute-start(bf16[1,1536]{1,0:T(2,128)(2,1)S(1)} %bitcast.165), channel_id=1, source_target_pairs={{0,4},{4,8},{8,12},{1,5},{5,9},{9,13},{2,6},{6,10},{10,14},{3,7},{... | collective-permute-start | bytes 9224 | tf_op jit(solution)/shard_map/ppermute | solution.py:16
  114.2 5.5 %collective-permute-start.3 = (bf16[1,1536]{1,0:T(2,128)(2,1)S(1)}, bf16[1,1536]{1,0:T(2,128)(2,1)S(1)}, u32[]{:S(2)}, u32[]{:S(2)}) collective-permute-start(bf16[1,1536]{1,0:T(2,128)(2,1)S(1)} %bitcast.166), channel_id=1, source_target_pairs={{4,0},{8,4},{12,8},{5,1},{9,5},{13,9},{6,2},{10,6},{14,10},{7,3},{... | collective-permute-start | bytes 9224 | tf_op jit(solution)/shard_map/ppermute | solution.py:17
  124.0 5.6 %copy-start.9 = (f32[64,6]{0,1:T(8,128)S(1)}, f32[64,6]{0,1:T(8,128)}, u32[]{:S(2)}) copy-start(f32[64,6]{0,1:T(8,128)} %copy-done.8) | copy-start | bytes 4612
  124.0 5.6 %copy-start.11 = (f32[64,6]{0,1:T(8,128)S(1)}, f32[64,6]{0,1:T(8,128)}, u32[]{:S(2)}) copy-start(f32[64,6]{0,1:T(8,128)} %copy-done.10) | copy-start | bytes 4612
  126.0 47.4 %copy-start.13 = (pred[256]{0:T(512)(128)(4,1)S(1)}, pred[256]{0:T(512)(128)(4,1)}, u32[]{:S(2)}) copy-start(pred[256]{0:T(512)(128)(4,1)} %copy-done.12) | copy-start | bytes 772
  129.5 85.5 %all-reduce.11.cloned.1.call-start = ((), (), s32[]{:S(2)}) async-start(), calls=%async_computation.3 | async-start | bytes 393216 | tf_op jit(solution)/shard_map/psum | solution.py:23
  159.9 6.7 %collective-permute-start.4 = (bf16[64,6,64]{0,2,1:T(8,128)(2,1)}, bf16[64,6,64]{0,2,1:T(8,128)(2,1)}, u32[]{:S(2)}, u32[]{:S(2)}) collective-permute-start(bf16[64,6,64]{0,2,1:T(8,128)(2,1)} %bitcast.18), channel_id=1, source_target_pairs={{0,4},{4,8},{8,12},{12,0},{1,5},{5,9},{9,13},{13,1},{2,6},{6,10},{... | collective-permute-start | bytes 147464 | tf_op jit(solution)/shard_map/ppermute | solution.py:140
  166.6 6.8 %collective-permute-start.5 = (bf16[64,6,64]{0,2,1:T(8,128)(2,1)}, bf16[64,6,64]{0,2,1:T(8,128)(2,1)}, u32[]{:S(2)}, u32[]{:S(2)}) collective-permute-start(bf16[64,6,64]{0,2,1:T(8,128)(2,1)} %collective-permute-done.4), channel_id=1, source_target_pairs={{0,4},{4,8},{8,12},{12,0},{1,5},{5,9},{9,13},{13,1},{2,6},{6,10},{... | collective-permute-start | bytes 147464 | tf_op jit(solution)/shard_map/ppermute | solution.py:140
  173.4 15.4 %collective-permute-start.6 = (bf16[64,6,64]{0,2,1:T(8,128)(2,1)}, bf16[64,6,64]{0,2,1:T(8,128)(2,1)}, u32[]{:S(2)}, u32[]{:S(2)}) collective-permute-start(bf16[64,6,64]{0,2,1:T(8,128)(2,1)} %collective-permute-done.5), channel_id=1, source_target_pairs={{0,4},{4,8},{8,12},{12,0},{1,5},{5,9},{9,13},{13,1},{2,6},{6,10},{... | collective-permute-start | bytes 147464 | tf_op jit(solution)/shard_map/ppermute | solution.py:140
  193.1 21.9 %copy-start.4 = (f32[64,768]{1,0:T(8,128)S(1)}, f32[64,768]{1,0:T(8,128)}, u32[]{:S(2)}) copy-start(f32[64,768]{1,0:T(8,128)} %all-reduce.9.cloned.1.call-done) | copy-start | bytes 589828
Sparse Core Ops, SparseCore 0:
  53.1 18.4 all-reduce.4
  88.4 18.2 all-reduce.6
  129.6 18.0 all-reduce.8
  195.5 19.4 all-reduce.10
